TPU v7x, 32 devices: a whole 2x2x4 slice. The times are simulated.
32 devices in a mesh: batch: 2 (over y), gy: 4 (over z), gx: 4 (over x, core).
Axes of the slice: x: 2, y: 2, z: 4, core: 2. Of those that a mesh axis runs over, the one named last changes fastest.
Arguments:
- x_fine: bfloat16 [2, 32, 128, 256], P('batch', 'gy', 'gx'), may hold values from -6 to 6
- dy_fine: bfloat16 [2, 32, 128, 256], P('batch', 'gy', 'gx'), may hold values from -6 to 6
- x_coarse: bfloat16 [2, 16, 16, 1024], P('batch', 'gy', 'gx'), may hold values from -6 to 6
- dy_coarse: bfloat16 [2, 16, 16, 1024], P('batch', 'gy', 'gx'), may hold values from -6 to 6
- timestep: int32 [2], P('batch'), may hold values from 0 to 999
- fine_gain: float32 [256], replicated, may hold values from 0.5 to 2.5, as said below
- coarse_gain: float32 [1024], replicated, may hold values from 0.5 to 2.5, as said below
- fine_qkv: bfloat16 [256, 768], replicated, may hold values from -0.375 to 0.375
- fine_out: bfloat16 [256, 256], replicated, may hold values from -0.375 to 0.375
- coarse_qkv: bfloat16 [3, 1024, 1024], P(None, ('gy', 'gx')), may hold values from -0.1875 to 0.1875
- coarse_out: bfloat16 [1024, 1024], P(('gy', 'gx')), may hold values from -0.1875 to 0.1875
Outputs:
- dx_fine: bfloat16 [2, 32, 128, 256], P('batch', 'gy', 'gx')
- dx_coarse: bfloat16 [2, 16, 16, 1024], P('batch', 'gy', 'gx')
- grad_fine_qkv: bfloat16 [256, 768], replicated
- grad_fine_out: bfloat16 [256, 256], replicated
- grad_coarse_qkv: bfloat16 [3, 1024, 1024], P(None, ('gy', 'gx'))
- grad_coarse_out: bfloat16 [1024, 1024], P(('gy', 'gx'))
Inputs may be any that keep to these rules, and one draw needn't show every extreme that they name: `fine_gain`: the norm gains are positive. `coarse_gain`: the norm gains are positive.
All inputs are finite; a program needn't handle non-finite values.
Results may differ from a plain program's by a relative error of at most 0.017.
The roundings to bfloat16 on the way count: a program that leaves them out, or rounds other values in their place, can miss the bound.
Values may be sent and summed in bfloat16 or wider, within the bound.
No kernel may reach another device: no remote copies, remote signals or barrier semaphores. Data moves between devices by JAX's collectives and lax.ppermute only.
A program may use at most 64 MiB of HBM per device.

v0:
```python
import math

import jax
import jax.numpy as jnp
from jax import lax
from jax.sharding import PartitionSpec as P

D_F = 256
H_F = 4
D_C = 1024
HD = 64
RAD = 3


eps = 1e-06
log_span = math.log(1000.0)
block_side = 8


def padded_2(array, sides, width):
    for axis, dim in sides:
        peers, length = (lax.axis_size(axis), array.shape[dim])
        up = [(i, (i + 1) % peers) for i in range(peers - 1)]
        down = [(j, i) for i, j in up]
        last = lax.slice_in_dim(array, length - width, length, axis=dim)
        leading = lax.slice_in_dim(array, 0, width, axis=dim)
        before = lax.ppermute(last, axis, up)
        after = lax.ppermute(leading, axis, down)
        array = jnp.concatenate([before, array, after], axis=dim)
    return array


def shifted(value, axis, steps):
    count = lax.axis_size(axis)
    leading, last = (max(0, -steps), min(count, count - steps))
    return lax.ppermute(value, axis, [(source, source + steps) for source in range(leading, last)])


def contract(pattern, first_op, second_op):
    return jnp.einsum(pattern, first_op, second_op, preferred_element_type=jnp.float32)


def score_scale():
    return 1.0 / math.sqrt(HD)


def time_gain(gains, step_value):
    channels = gains.shape[0]
    frequency = jnp.exp(-log_span * jnp.arange(channels, dtype=jnp.float32) / channels)
    return gains * (1.0 + 0.5 * jnp.cos(step_value.astype(jnp.float32) * frequency))


def norm_forward(source, factor):
    floats = source.astype(jnp.float32)
    inverse = lax.rsqrt(jnp.mean(floats * floats, axis=-1, keepdims=True) + eps)
    return ((floats * inverse * factor).astype(jnp.bfloat16), inverse)


def norm_backward(source, inverse, factor, upstream):
    floats = source.astype(jnp.float32)
    scaled = upstream * factor
    middle = jnp.mean(floats * scaled, axis=-1, keepdims=True)
    return (inverse * scaled - floats * inverse * inverse * inverse * middle).astype(jnp.bfloat16)


def to_tiles(planar):
    height, breadth, channels = planar.shape
    pieces = planar.reshape(
        height // block_side, block_side, breadth // block_side, block_side, channels
    )
    return pieces.transpose(0, 2, 1, 3, 4).reshape(-1, block_side * block_side, channels)


def from_tiles(blocks, height, breadth):
    channels = blocks.shape[-1]
    pieces = blocks.reshape(
        height // block_side, breadth // block_side, block_side, block_side, channels
    )
    return pieces.transpose(0, 2, 1, 3, 4).reshape(height, breadth, channels)


def windows(padded, height, breadth):
    extent = block_side + 2 * RAD
    block_rows = height // block_side
    across = breadth // block_side
    channels = padded.shape[-1]
    widened = jnp.pad(
        padded,
        (
            (0, (block_rows + 1) * block_side - padded.shape[0]),
            (0, (across + 1) * block_side - padded.shape[1]),
            (0, 0),
        ),
    )
    blocks_grid = widened.reshape(
        block_rows + 1, block_side, across + 1, block_side, channels
    ).transpose(0, 2, 1, 3, 4)
    upper_pair = jnp.concatenate([blocks_grid[:-1, :-1], blocks_grid[:-1, 1:]], axis=3)
    lower_pair = jnp.concatenate([blocks_grid[1:, :-1], blocks_grid[1:, 1:]], axis=3)
    square = jnp.concatenate([upper_pair, lower_pair], axis=2)
    return square[:, :, :extent, :extent].reshape(block_rows * across, extent * extent, channels)


def intersection_add(windowed, height, breadth):
    extent = block_side + 2 * RAD
    block_rows = height // block_side
    across = breadth // block_side
    channels = windowed.shape[-1]
    layout = windowed.reshape(block_rows, across, extent, extent, channels)
    layout = jnp.pad(
        layout, ((0, 0), (0, 0), (0, 2 * block_side - extent), (0, 2 * block_side - extent), (0, 0))
    )
    summed = jnp.zeros((block_rows + 1, across + 1, block_side, block_side, channels), jnp.float32)
    for row_half in range(2):
        for col_half in range(2):
            quarter = layout[
                :,
                :,
                row_half * block_side : (row_half + 1) * block_side,
                col_half * block_side : (col_half + 1) * block_side,
            ]
            summed = summed + jnp.pad(
                quarter,
                ((row_half, 1 - row_half), (col_half, 1 - col_half), (0, 0), (0, 0), (0, 0)),
            )
    merged = summed.transpose(0, 2, 1, 3, 4).reshape(
        (block_rows + 1) * block_side, (across + 1) * block_side, channels
    )
    return merged[: height + 2 * RAD, : breadth + 2 * RAD]


def pair_mask():
    extent = block_side + 2 * RAD
    inner_pos = jnp.arange(block_side * block_side)
    outer_pos = jnp.arange(extent * extent)
    row_gap = outer_pos[None, :] // extent - inner_pos[:, None] // block_side
    col_gap = outer_pos[None, :] % extent - inner_pos[:, None] % block_side
    return (row_gap >= 0) & (row_gap <= 2 * RAD) & (col_gap >= 0) & (col_gap <= 2 * RAD)


def fine_forward(queries, key_values, valid_pad):
    height, breadth, channels = queries.shape
    query_blocks = to_tiles(queries)
    block_count = query_blocks.shape[0]
    query_heads = query_blocks.reshape(block_count, -1, H_F, HD)
    key_windows = windows(key_values, height, breadth)
    key_heads = key_windows[..., :channels].reshape(block_count, -1, H_F, HD)
    value_heads = key_windows[..., channels:].reshape(block_count, -1, H_F, HD)
    allowed = (
        pair_mask()[None, None]
        & windows(valid_pad[..., None], height, breadth)[:, None, None, :, 0]
    )
    scores = contract("bqhe,bkhe->bhqk", query_heads, key_heads) * score_scale()
    scores = jnp.where(allowed, scores, -1e30)
    peak = jnp.max(scores, axis=-1, keepdims=True)
    log_total = peak + jnp.log(jnp.sum(jnp.exp(scores - peak), axis=-1, keepdims=True))
    shares = jnp.where(allowed, jnp.exp(scores - log_total), 0.0)
    weights = shares.astype(jnp.bfloat16)
    mixed = contract("bhqk,bkhe->bqhe", weights, value_heads).astype(jnp.bfloat16)
    attended = from_tiles(mixed.reshape(block_count, -1, channels), height, breadth)
    return (attended, query_heads, key_heads, value_heads, shares, weights, log_total)


def fine_query_backward(upstream, query_heads, key_heads, value_heads, shares, height, breadth):
    block_count = query_heads.shape[0]
    upward_heads = to_tiles(upstream).reshape(block_count, -1, H_F, HD)
    products = contract("bqhe,bkhe->bhqk", upward_heads, value_heads)
    centre = jnp.sum(shares * products, axis=-1, keepdims=True)
    slopes = (shares * (products - centre)).astype(jnp.bfloat16)
    grad_query = contract("bhqk,bkhe->bqhe", slopes, key_heads) * score_scale()
    grad_query = from_tiles(grad_query.reshape(block_count, -1, H_F * HD), height, breadth)
    return (grad_query, upward_heads, slopes, centre)


def key_grads_windows(slopes, weights, query_heads, upward_heads):
    block_count = query_heads.shape[0]
    grad_key = contract("bhqk,bqhe->bkhe", slopes, query_heads).reshape(block_count, -1, D_F)
    grad_value = contract("bhqk,bqhe->bkhe", weights, upward_heads).reshape(block_count, -1, D_F)
    return jnp.concatenate([grad_key, grad_value], axis=-1)


def local(
    x_fine,
    dy_fine,
    x_coarse,
    dy_coarse,
    timestep,
    fine_gain,
    coarse_gain,
    fine_qkv,
    fine_out,
    coarse_qkv,
    coarse_out,
):
    step_value = timestep[0]
    picture = x_fine[0]
    height, breadth = (picture.shape[0], picture.shape[1])
    factor = time_gain(fine_gain, step_value)
    normed, inverse = norm_forward(picture, factor)
    flat_normed = normed.reshape(-1, D_F)
    projected = (
        jnp.dot(flat_normed, fine_qkv, preferred_element_type=jnp.float32)
        .astype(jnp.bfloat16)
        .reshape(height, breadth, 3 * D_F)
    )
    queries = projected[..., :D_F]
    key_values = projected[..., D_F:]
    kv_pad = padded_2(key_values[None], (("gy", 1), ("gx", 2)), RAD)[0]
    row_first = lax.axis_index("gy") * height - RAD
    col_first = lax.axis_index("gx") * breadth - RAD
    pad_rows = row_first + jnp.arange(height + 2 * RAD, dtype=jnp.int32)
    pad_cols = col_first + jnp.arange(breadth + 2 * RAD, dtype=jnp.int32)
    rows_inside = (pad_rows >= 0) & (pad_rows < height * lax.axis_size("gy"))
    cols_inside = (pad_cols >= 0) & (pad_cols < breadth * lax.axis_size("gx"))
    valid_pad = rows_inside[:, None] & cols_inside[None, :]
    attended, query_heads, key_heads, value_heads, shares, weights, log_total = fine_forward(
        queries, kv_pad, valid_pad
    )
    flat_cot = dy_fine[0].reshape(-1, D_F)
    grad_out_local = lax.dot_general(
        attended.reshape(-1, D_F),
        flat_cot,
        (((0,), (0,)), ((), ())),
        preferred_element_type=jnp.float32,
    )
    upstream = (
        lax.dot_general(
            flat_cot, fine_out, (((1,), (1,)), ((), ())), preferred_element_type=jnp.float32
        )
        .astype(jnp.bfloat16)
        .reshape(height, breadth, D_F)
    )
    grad_query, upward_heads, slopes, centre = fine_query_backward(
        upstream, query_heads, key_heads, value_heads, shares, height, breadth
    )
    summed = intersection_add(
        key_grads_windows(slopes, weights, query_heads, upward_heads), height, breadth
    )
    from_left = shifted(summed[:, breadth + RAD :], "gx", 1)
    from_right = shifted(summed[:, :RAD], "gx", -1)
    middle = summed[:, RAD : breadth + RAD]
    middle = middle.at[:, :RAD].add(from_left)
    middle = middle.at[:, breadth - RAD :].add(from_right)
    from_above = shifted(middle[height + RAD :], "gy", 1)
    from_below = shifted(middle[:RAD], "gy", -1)
    key_grads = middle[RAD : height + RAD]
    key_grads = key_grads.at[:RAD].add(from_above)
    key_grads = key_grads.at[height - RAD :].add(from_below)
    grad_proj = (
        jnp.concatenate(
            [grad_query, key_grads[..., :D_F] * score_scale(), key_grads[..., D_F:]], axis=-1
        )
        .astype(jnp.bfloat16)
        .reshape(-1, 3 * D_F)
    )
    grad_qkv_local = lax.dot_general(
        flat_normed, grad_proj, (((0,), (0,)), ((), ())), preferred_element_type=jnp.float32
    )
    down_grad = lax.dot_general(
        grad_proj, fine_qkv, (((1,), (1,)), ((), ())), preferred_element_type=jnp.float32
    ).reshape(height, breadth, D_F)
    dx_picture = norm_backward(picture, inverse, factor, down_grad)
    coarse_tokens = x_coarse[0].reshape(-1, D_C)
    coarse_factor = time_gain(coarse_gain, step_value)
    coarse_normed, coarse_inverse = norm_forward(coarse_tokens, coarse_factor)
    coarse_cot = dy_coarse[0].reshape(-1, D_C)
    all_normed = lax.all_gather(coarse_normed, ("gy", "gx"), axis=0, tiled=True)
    coarse_proj = contract("td,khd->kth", all_normed, coarse_qkv).astype(jnp.bfloat16)
    head_queries, head_keys, head_values = (coarse_proj[0], coarse_proj[1], coarse_proj[2])
    coarse_scores = contract("te,se->ts", head_queries, head_keys) * score_scale()
    coarse_peak = jnp.max(coarse_scores, axis=-1, keepdims=True)
    coarse_log = coarse_peak + jnp.log(
        jnp.sum(jnp.exp(coarse_scores - coarse_peak), axis=-1, keepdims=True)
    )
    coarse_shares = jnp.exp(coarse_scores - coarse_log)
    coarse_weights = coarse_shares.astype(jnp.bfloat16)
    head_mixed = contract("ts,se->te", coarse_weights, head_values).astype(jnp.bfloat16)
    all_cot = lax.all_gather(coarse_cot, ("gy", "gx"), axis=0, tiled=True)
    head_upstream = contract("td,ed->te", all_cot, coarse_out).astype(jnp.bfloat16)
    coarse_out_local = contract("te,td->ed", head_mixed, all_cot)
    coarse_products = contract("te,se->ts", head_upstream, head_values)
    coarse_centre = jnp.sum(coarse_shares * coarse_products, axis=-1, keepdims=True)
    coarse_slopes = (coarse_shares * (coarse_products - coarse_centre)).astype(jnp.bfloat16)
    head_grad_query = (contract("ts,se->te", coarse_slopes, head_keys) * score_scale()).astype(
        jnp.bfloat16
    )
    head_grad_key = (contract("ts,te->se", coarse_slopes, head_queries) * score_scale()).astype(
        jnp.bfloat16
    )
    head_grad_value = contract("ts,te->se", coarse_weights, head_upstream).astype(jnp.bfloat16)
    stacked = jnp.stack([head_grad_query, head_grad_key, head_grad_value])
    coarse_qkv_local = contract("kte,td->ked", stacked, all_normed)
    head_part = contract("kte,ked->td", stacked, coarse_qkv)
    coarse_down = lax.psum_scatter(
        head_part.astype(jnp.bfloat16), ("gy", "gx"), scatter_dimension=0, tiled=True
    ).astype(jnp.float32)
    dx_coarse_tok = norm_backward(coarse_tokens, coarse_inverse, coarse_factor, coarse_down)
    fine_qkv_sum, fine_out_sum = lax.psum((grad_qkv_local, grad_out_local), ("batch", "gy", "gx"))
    coarse_qkv_sum, coarse_out_sum = lax.psum((coarse_qkv_local, coarse_out_local), "batch")
    return (
        dx_picture[None],
        dx_coarse_tok.reshape(x_coarse.shape),
        fine_qkv_sum.astype(jnp.bfloat16),
        fine_out_sum.astype(jnp.bfloat16),
        coarse_qkv_sum.astype(jnp.bfloat16),
        coarse_out_sum.astype(jnp.bfloat16),
    )


def solution(mesh):
    placed = (
        P("batch", "gy", "gx", None),
        P("batch", "gy", "gx", None),
        P("batch", "gy", "gx", None),
        P("batch", "gy", "gx", None),
        P("batch"),
        P(),
        P(),
        P(),
        P(),
        P(None, ("gy", "gx"), None),
        P(("gy", "gx"), None),
    )
    return jax.shard_map(
        local,
        mesh=mesh,
        in_specs=placed,
        out_specs=(
            P("batch", "gy", "gx", None),
            P("batch", "gy", "gx", None),
            P(),
            P(),
            P(None, ("gy", "gx"), None),
            P(("gy", "gx"), None),
        ),
        check_vma=False,
    )
```

profile of v0, /device:TPU:0, one launch (start us, length us, event | category | flops | bytes accessed | tf_op | source)
XLA Modules:
  0.0 205.2 jit_solution(4602646157763296801)
XLA Ops:
  7.9 1.0 fusion.28
  9.1 0.5 copy-done.14
  9.6 0.7 add_multiply_fusion.1
  10.3 1.0 fusion.20
  11.3 1.3 convolution_convert_fusion
  12.7 5.1 %collective-permute-start = (bf16[1,3,32,512]{3,2,1,0:T(8,128)(2,1)S(1)}, bf16[1,3,32,512]{3,2,1,0:T(8,128)(2,1)S(1)}, u32[]{:S(2)}, u32[]{:S(2)}) collective-permute-start(bf16[1,3,32,512]{3,2,1,0:T(8,128)(2,1)S(1)} %get-tuple-element.74), channel_id=1, source_target_pairs={{0,4},{4,8},{8,12},{1,5},{5,9},{9,13},{2,6},{6,10},{10,14},{3,7},{... | collective-permute-start | bytes 294920 | tf_op jit(solution)/shard_map/ppermute | solution.py:27
  17.7 1.3 collective-permute-start.1
  19.4 24.3 %all_gather.6 = bf16[256,1024]{1,0:T(8,128)(2,1)S(1)} all-gather(bf16[16,1024]{1,0:T(8,128)(2,1)S(1)} %multiply_convert_fusion.2), channel_id=1, replica_groups=mesh['batch'=2,'gy'=4,'gx'=4] {'gy','gx'}, dimensions={0}, use_global_device_ids=true | all-gather | bytes 557056 | tf_op jit(solution)/shard_map/all_gather | solution.py:267
  43.7 0.3 fusion.5
  44.1 0.3 fusion.63
  44.4 18.9 %all_gather.7 = bf16[256,1024]{1,0:T(8,128)(2,1)S(1)} all-gather(bf16[16,1024]{1,0:T(8,128)(2,1)S(1)} %reshape_squeeze.8), channel_id=1, replica_groups=mesh['batch'=2,'gy'=4,'gx'=4] {'gy','gx'}, dimensions={0}, use_global_device_ids=true | all-gather | bytes 557056 | tf_op jit(solution)/shard_map/all_gather | solution.py:278
  63.3 0.3 convolution_convert_fusion.6
  63.6 0.2 fusion.8
  63.8 0.3 multiply_reduce_fusion.1
  64.5 1.1 fusion.1
  65.7 0.4 fusion.9
  66.0 0.3 fusion.14
  66.6 0.2 convolution_convert_fusion.2
  66.8 30.6 %all-reduce.11 = (bf16[3,64,1024]{2,1,0:T(8,128)(2,1)}, bf16[64,1024]{1,0:T(8,128)(2,1)}) all-reduce(f32[3,64,1024]{2,1,0:T(8,128)S(1)} %fusion.14, f32[64,1024]{1,0:T(8,128)S(1)} %fusion.9), channel_id=1, replica_groups=mesh['batch'=2,'gy'=4,'gx'=4] {'batch'}, use_global_device_ids=true, to_apply=%region_13.14 | all-reduce | flops 262144 | bytes 1572864 | tf_op jit(solution)/shard_map/psum | solution.py:299
  97.7 1.3 collective-permute-start.2
  99.0 1.5 collective-permute-start.3
  101.3 2.8 %collective-permute-done.3 = bf16[1,14,3,512]{3,2,1,0:T(4,128)(2,1)S(1)} collective-permute-done((bf16[1,14,3,512]{3,2,1,0:T(4,128)(2,1)S(1)}, bf16[1,14,3,512]{3,2,1,0:T(4,128)(2,1)S(1)}, u32[]{:S(2)}, u32[]{:S(2)}) %collective-permute-start.3) | collective-permute-done | bytes 43040 | tf_op jit(solution)/shard_map/ppermute | solution.py:28
  104.1 0.2 maximum_bitcast_fusion
  104.6 0.7 copy.38
  105.3 0.3 fusion.58
  105.6 0.3 copy.39
  105.9 0.3 copy.44
  106.2 0.4 fusion.62
  106.6 0.4 exponential_reduce_fusion
  107.1 0.4 fusion.3
  107.5 0.6 multiply_reduce_fusion
  108.1 0.4 convolution_bitcast_fusion.1
  108.5 0.4 multiply_convert_fusion
  108.8 1.0 fusion.4
  109.9 1.3 convolution_bitcast_fusion.2
  111.3 0.2 reshape_reshape.23
  111.5 2.0 copy.49
  113.6 1.9 concatenate.57
  115.5 1.1 copy.51
  116.6 1.9 concatenate.58
  118.7 0.9 copy-done.2
  119.9 0.4 fusion.55
  120.3 0.4 add_bitcast_fusion
  120.8 1.0 copy.52
  121.8 0.7 fusion.56
  122.5 5.4 %collective-permute-start.4 = (f32[14,3,512]{2,1,0:T(4,128)}, f32[14,3,512]{2,1,0:T(4,128)}, u32[]{:S(2)}, u32[]{:S(2)}) collective-permute-start(f32[14,3,512]{2,1,0:T(4,128)} %get-tuple-element.63), channel_id=1, source_target_pairs={{0,1},{1,2},{2,3},{4,5},{5,6},{6,7},{8,9},{9,10},{10,11},{12,13},{... | collective-permute-start | bytes 258056 | tf_op jit(solution)/shard_map/ppermute | solution.py:36
  127.9 0.9 fusion.64
  129.2 0.2 reshape_reshape.22
  129.4 1.3 collective-permute-start.5
  130.7 0.9 slice_add_fusion.3
  131.7 0.4 scatter-add.14
  132.1 0.6 collective-permute-done.5
  132.7 0.3 scatter-add.15
  133.1 1.4 collective-permute-start.6
  134.6 1.3 collective-permute-start.7
  135.9 2.3 %collective-permute-done.6 = f32[3,32,512]{2,1,0:T(8,128)S(1)} collective-permute-done((f32[3,32,512]{2,1,0:T(8,128)S(1)}, f32[3,32,512]{2,1,0:T(8,128)S(1)}, u32[]{:S(2)}, u32[]{:S(2)}) %collective-permute-start.6) | collective-permute-done | bytes 196640 | tf_op jit(solution)/shard_map/ppermute | solution.py:36
  138.2 4.7 %collective-permute-done.7 = f32[3,32,512]{2,1,0:T(8,128)S(1)} collective-permute-done((f32[3,32,512]{2,1,0:T(8,128)S(1)}, f32[3,32,512]{2,1,0:T(8,128)S(1)}, u32[]{:S(2)}, u32[]{:S(2)}) %collective-permute-start.7) | collective-permute-done | bytes 196640 | tf_op jit(solution)/shard_map/ppermute | solution.py:36
  143.0 0.4 fusion.29
  143.5 0.4 convolution_bitcast_fusion.3
  143.9 0.8 fusion.34
  144.7 51.3 %all-reduce.12 = (bf16[256,768]{1,0:T(8,128)(2,1)}, bf16[256,256]{1,0:T(8,128)(2,1)}) all-reduce(f32[256,768]{1,0:T(8,128)S(1)} %convolution_bitcast_fusion.3, f32[256,256]{1,0:T(8,128)S(1)} %copy-done.5), channel_id=1, replica_groups=mesh['batch'=2,'gy'=4,'gx'=4] {'batch','gy','gx'}, use_global_device_ids=true, to_apply=%region_11.12 | all-reduce | flops 262144 | bytes 1572864 | tf_op jit(solution)/shard_map/psum | solution.py:298
  196.0 0.9 multiply_reduce_fusion.2
  196.9 0.8 subtract_convert_fusion
  197.7 0.6 reshape.470
  (106 shorter events, 3.9 us)
Async XLA Ops:
  7.2 36.6 %copy-start = (bf16[3,64,1024]{2,1,0:T(8,128)(2,1)S(1)}, bf16[3,64,1024]{2,1,0:T(8,128)(2,1)}, u32[]{:S(2)}) copy-start(bf16[3,64,1024]{2,1,0:T(8,128)(2,1)} %param.28) | copy-start | bytes 1179652
  7.2 11.9 %copy-start.10 = (bf16[1,4,4,1024]{3,2,1,0:T(4,128)(2,1)S(1)}, bf16[1,4,4,1024]{3,2,1,0:T(4,128)(2,1)}, u32[]{:S(2)}) copy-start(bf16[1,4,4,1024]{3,2,1,0:T(4,128)(2,1)} %param.21) | copy-start | bytes 98308
  7.2 12.1 %copy-start.21 = (f32[1024]{0:T(1024)S(1)}, f32[1024]{0:T(1024)}, u32[]{:S(2)}) copy-start(f32[1024]{0:T(1024)} %param.25) | copy-start | bytes 12292
  7.2 12.1 %copy-start.16 = (bf16[1,4,4,1024]{3,2,1,0:T(4,128)(2,1)S(1)}, bf16[1,4,4,1024]{3,2,1,0:T(4,128)(2,1)}, u32[]{:S(2)}) copy-start(bf16[1,4,4,1024]{3,2,1,0:T(4,128)(2,1)} %param.22) | copy-start | bytes 98308
  7.2 188.8 %reduce-scatter.2.cloned.1.call-start = ((), (), s32[]{:S(2)}) async-start(), calls=%async_computation.1 | async-start | bytes 557056 | tf_op jit(solution)/shard_map/reduce_scatter | solution.py:294
  9.0 0.6 copy-start.14
  10.3 33.4 %copy-start.19 = (f32[256]{0:T(256)}, f32[256]{0:T(256)S(1)}, u32[]{:S(2)}) copy-start(f32[256]{0:T(256)S(1)} %add_multiply_fusion.1) | copy-start | bytes 3076
  12.7 50.6 %copy-start.11 = (bf16[64,1024]{1,0:T(8,128)(2,1)S(1)}, bf16[64,1024]{1,0:T(8,128)(2,1)}, u32[]{:S(2)}) copy-start(bf16[64,1024]{1,0:T(8,128)(2,1)} %param.29) | copy-start | bytes 393220
  12.7 85.0 %collective-permute-start = (bf16[1,3,32,512]{3,2,1,0:T(8,128)(2,1)S(1)}, bf16[1,3,32,512]{3,2,1,0:T(8,128)(2,1)S(1)}, u32[]{:S(2)}, u32[]{:S(2)}) collective-permute-start(bf16[1,3,32,512]{3,2,1,0:T(8,128)(2,1)S(1)} %get-tuple-element.74), channel_id=1, source_target_pairs={{0,4},{4,8},{8,12},{1,5},{5,9},{9,13},{2,6},{6,10},{10,14},{3,7},{... | collective-permute-start | bytes 294920 | tf_op jit(solution)/shard_map/ppermute | solution.py:27
  17.7 79.9 %collective-permute-start.1 = (bf16[1,3,32,512]{3,2,1,0:T(8,128)(2,1)S(1)}, bf16[1,3,32,512]{3,2,1,0:T(8,128)(2,1)S(1)}, u32[]{:S(2)}, u32[]{:S(2)}) collective-permute-start(bf16[1,3,32,512]{3,2,1,0:T(8,128)(2,1)S(1)} %get-tuple-element.75), channel_id=1, source_target_pairs={{4,0},{8,4},{12,8},{5,1},{9,5},{13,9},{6,2},{10,6},{14,10},{7,3},{... | collective-permute-start | bytes 294920 | tf_op jit(solution)/shard_map/ppermute | solution.py:28
  19.3 24.5 %copy-start.17 = (f32[16]{0:T(128)}, f32[16]{0:T(128)S(1)}, u32[]{:S(2)}) copy-start(f32[16]{0:T(128)S(1)} %rsqrt.26) | copy-start | bytes 196
  19.3 44.2 %copy-start.12 = (f32[1024]{0:T(1024)}, f32[1024]{0:T(1024)S(1)}, u32[]{:S(2)}) copy-start(f32[1024]{0:T(1024)S(1)} %add_multiply_fusion) | copy-start | bytes 12292
  65.6 1.0 copy-start.6
  65.6 1.0 copy-start.9
  97.7 3.6 %collective-permute-start.2 = (bf16[1,14,3,512]{3,2,1,0:T(4,128)(2,1)S(1)}, bf16[1,14,3,512]{3,2,1,0:T(4,128)(2,1)S(1)}, u32[]{:S(2)}, u32[]{:S(2)}) collective-permute-start(bf16[1,14,3,512]{3,2,1,0:T(4,128)(2,1)S(1)} %get-tuple-element.72), channel_id=1, source_target_pairs={{0,1},{1,2},{2,3},{4,5},{5,6},{6,7},{8,9},{9,10},{10,11},{12,13},{... | collective-permute-start | bytes 129032 | tf_op jit(solution)/shard_map/ppermute | solution.py:27
  99.0 5.1 %collective-permute-start.3 = (bf16[1,14,3,512]{3,2,1,0:T(4,128)(2,1)S(1)}, bf16[1,14,3,512]{3,2,1,0:T(4,128)(2,1)S(1)}, u32[]{:S(2)}, u32[]{:S(2)}) collective-permute-start(bf16[1,14,3,512]{3,2,1,0:T(4,128)(2,1)S(1)} %get-tuple-element.73), channel_id=1, source_target_pairs={{1,0},{2,1},{3,2},{5,4},{6,5},{7,6},{9,8},{10,9},{11,10},{13,12},{... | collective-permute-start | bytes 129032 | tf_op jit(solution)/shard_map/ppermute | solution.py:28
  116.6 1.9 copy-start.1
  118.5 1.1 copy-start.2
  120.7 7.2 %copy-start.7 = (bf16[1,8,32,256]{3,2,1,0:T(8,128)(2,1)S(1)}, bf16[1,8,32,256]{3,2,1,0:T(8,128)(2,1)}, u32[]{:S(2)}) copy-start(bf16[1,8,32,256]{3,2,1,0:T(8,128)(2,1)} %param.20) | copy-start | bytes 393220
  121.8 7.2 %copy-start.4 = (bf16[4,64,4,64]{1,3,2,0:T(8,128)(2,1)S(1)}, bf16[4,64,4,64]{1,3,2,0:T(8,128)(2,1)}, u32[]{:S(2)}) copy-start(bf16[4,64,4,64]{1,3,2,0:T(8,128)(2,1)} %fusion.4) | copy-start | bytes 393220
  122.5 8.2 %collective-permute-start.4 = (f32[14,3,512]{2,1,0:T(4,128)}, f32[14,3,512]{2,1,0:T(4,128)}, u32[]{:S(2)}, u32[]{:S(2)}) collective-permute-start(f32[14,3,512]{2,1,0:T(4,128)} %get-tuple-element.63), channel_id=1, source_target_pairs={{0,1},{1,2},{2,3},{4,5},{5,6},{6,7},{8,9},{9,10},{10,11},{12,13},{... | collective-permute-start | bytes 258056 | tf_op jit(solution)/shard_map/ppermute | solution.py:36
  129.4 3.2 %collective-permute-start.5 = (f32[14,3,512]{2,1,0:T(4,128)S(1)}, f32[14,3,512]{2,1,0:T(4,128)S(1)}, u32[]{:S(2)}, u32[]{:S(2)}) collective-permute-start(f32[14,3,512]{2,1,0:T(4,128)S(1)} %get-tuple-element.62), channel_id=1, source_target_pairs={{1,0},{2,1},{3,2},{5,4},{6,5},{7,6},{9,8},{10,9},{11,10},{13,12},{... | collective-permute-start | bytes 258056 | tf_op jit(solution)/shard_map/ppermute | solution.py:36
  133.0 10.0 %copy-start.3 = (bf16[1,8,32,256]{3,2,1,0:T(8,128)(2,1)S(1)}, bf16[1,8,32,256]{3,2,1,0:T(8,128)(2,1)}, u32[]{:S(2)}) copy-start(bf16[1,8,32,256]{3,2,1,0:T(8,128)(2,1)} %param.19) | copy-start | bytes 393220
  133.1 10.0 %copy-start.8 = (bf16[256,768]{1,0:T(8,128)(2,1)S(1)}, bf16[256,768]{1,0:T(8,128)(2,1)}, u32[]{:S(2)}) copy-start(bf16[256,768]{1,0:T(8,128)(2,1)} %param.26) | copy-start | bytes 1179652
  133.1 10.0 %copy-start.20 = (f32[256]{0:T(256)S(1)}, f32[256]{0:T(256)}, u32[]{:S(2)}) copy-start(f32[256]{0:T(256)} %copy-done.19) | copy-start | bytes 3076
  133.1 5.1 %collective-permute-start.6 = (f32[3,32,512]{2,1,0:T(8,128)S(1)}, f32[3,32,512]{2,1,0:T(8,128)S(1)}, u32[]{:S(2)}, u32[]{:S(2)}) collective-permute-start(f32[3,32,512]{2,1,0:T(8,128)S(1)} %get-tuple-element.65), channel_id=1, source_target_pairs={{0,4},{4,8},{8,12},{1,5},{5,9},{9,13},{2,6},{6,10},{10,14},{3,7},{... | collective-permute-start | bytes 589832 | tf_op jit(solution)/shard_map/ppermute | solution.py:36
  134.6 8.3 %collective-permute-start.7 = (f32[3,32,512]{2,1,0:T(8,128)S(1)}, f32[3,32,512]{2,1,0:T(8,128)S(1)}, u32[]{:S(2)}, u32[]{:S(2)}) collective-permute-start(f32[3,32,512]{2,1,0:T(8,128)S(1)} %get-tuple-element.64), channel_id=1, source_target_pairs={{4,0},{8,4},{12,8},{5,1},{9,5},{13,9},{6,2},{10,6},{14,10},{7,3},{... | collective-permute-start | bytes 589832 | tf_op jit(solution)/shard_map/ppermute | solution.py:36
  138.2 5.3 %copy-start.15 = (f32[8,32]{1,0:T(8,128)S(1)}, f32[8,32]{1,0:T(8,128)}, u32[]{:S(2)}) copy-start(f32[8,32]{1,0:T(8,128)} %copy-done.14) | copy-start | bytes 3076
  143.5 1.2 copy-start.5
  143.5 52.5 %copy-start.13 = (f32[1024]{0:T(1024)S(1)}, f32[1024]{0:T(1024)}, u32[]{:S(2)}) copy-start(f32[1024]{0:T(1024)} %copy-done.12) | copy-start | bytes 12292
  143.5 53.4 %copy-start.18 = (f32[16]{0:T(128)S(1)}, f32[16]{0:T(128)}, u32[]{:S(2)}) copy-start(f32[16]{0:T(128)} %copy-done.17) | copy-start | bytes 196
Sparse Core Ops, SparseCore 0:
  65.7 54.2 reduce-scatter.1
where the time goes:
time: 206 us; the launch traced here: 205 us
  blocking collectives  125 us (61%)
  starting transfers between devices  18.6 us (9%)
  local copies, waits for them, and re-layouts  16.3 us (8%)
  between operations  15.5 us (8%)
  matrix products  10.7 us (5%)
  waiting for transfers between devices  10.3 us (5%)
  other arithmetic  8.66 us (4%)
    psum x1, blocking collectives, local(): lax.psum((grad_qkv_local, grad_out_local), ('batch', 'gy', 'gx'))  51.3 us
    psum x1, blocking collectives, local(): lax.psum((coarse_qkv_local, coarse_out_local), 'batch')  30.6 us
    all_gather x1, blocking collectives, local(): all_normed = lax.all_gather(coarse_normed, ('gy', 'gx'), axis=0, tiled=True)  24.3 us
    all_gather x1, blocking collectives, local(): all_cot = lax.all_gather(coarse_cot, ('gy', 'gx'), axis=0, tiled=True)  18.9 us
    ppermute x4, starting transfers between devices, shifted(): lax.ppermute(value, axis, [(source, source + steps) for source in range(l...  9.42 us
    dot_general x16, matrix products, contract(): jnp.einsum(pattern, first_op, second_op, preferred_element_type=jnp.float32)  7.56 us
    ppermute x4, waiting for transfers between devices, shifted(): lax.ppermute(value, axis, [(source, source + steps) for source in range(l...  7.54 us
    ppermute x2, starting transfers between devices, padded_2(): before = lax.ppermute(last, axis, up)  6.36 us
  transfers between devices with their start and end apart: 9, of which 4 were waited for; matrix products, arithmetic and copies ran while one was open for 13% of the time, Pallas kernels for 0%

commit v1 on v0

--- a/solution.py
+++ b/solution.py
@@ -177,6 +177,14 @@
     grad_key = contract("bhqk,bqhe->bkhe", slopes, query_heads).reshape(block_count, -1, D_F)
     grad_value = contract("bhqk,bqhe->bkhe", weights, upward_heads).reshape(block_count, -1, D_F)
     return jnp.concatenate([grad_key, grad_value], axis=-1)
+
+
+def batch_sum(partial):
+    images = lax.axis_size("batch")
+    if images != 2:
+        return lax.psum(partial, "batch")
+    other = lax.ppermute(partial, "batch", [(0, 1), (1, 0)])
+    return partial.astype(jnp.float32) + other.astype(jnp.float32)
 
 
 def local(
@@ -262,9 +270,11 @@
     dx_picture = norm_backward(picture, inverse, factor, down_grad)
     coarse_tokens = x_coarse[0].reshape(-1, D_C)
     coarse_factor = time_gain(coarse_gain, step_value)
-    coarse_normed, coarse_inverse = norm_forward(coarse_tokens, coarse_factor)
-    coarse_cot = dy_coarse[0].reshape(-1, D_C)
-    all_normed = lax.all_gather(coarse_normed, ("gy", "gx"), axis=0, tiled=True)
+    own = jnp.concatenate([coarse_tokens, dy_coarse[0].reshape(-1, D_C)], axis=1)
+    everyone = lax.all_gather(own, ("gy", "gx"), axis=0, tiled=True)
+    all_normed, _ = norm_forward(everyone[:, :D_C], coarse_factor)
+    all_cot = everyone[:, D_C:]
+    _, coarse_inverse = norm_forward(coarse_tokens, coarse_factor)
     coarse_proj = contract("td,khd->kth", all_normed, coarse_qkv).astype(jnp.bfloat16)
     head_queries, head_keys, head_values = (coarse_proj[0], coarse_proj[1], coarse_proj[2])
     coarse_scores = contract("te,se->ts", head_queries, head_keys) * score_scale()
@@ -275,7 +285,6 @@
     coarse_shares = jnp.exp(coarse_scores - coarse_log)
     coarse_weights = coarse_shares.astype(jnp.bfloat16)
     head_mixed = contract("ts,se->te", coarse_weights, head_values).astype(jnp.bfloat16)
-    all_cot = lax.all_gather(coarse_cot, ("gy", "gx"), axis=0, tiled=True)
     head_upstream = contract("td,ed->te", all_cot, coarse_out).astype(jnp.bfloat16)
     coarse_out_local = contract("te,td->ed", head_mixed, all_cot)
     coarse_products = contract("te,se->ts", head_upstream, head_values)
@@ -291,12 +300,25 @@
     stacked = jnp.stack([head_grad_query, head_grad_key, head_grad_value])
     coarse_qkv_local = contract("kte,td->ked", stacked, all_normed)
     head_part = contract("kte,ked->td", stacked, coarse_qkv)
-    coarse_down = lax.psum_scatter(
-        head_part.astype(jnp.bfloat16), ("gy", "gx"), scatter_dimension=0, tiled=True
-    ).astype(jnp.float32)
+    shares_out = lax.all_to_all(
+        head_part.astype(jnp.bfloat16), ("gy", "gx"), split_axis=0, concat_axis=0, tiled=True
+    )
+    ranks = lax.axis_size(("gy", "gx"))
+    coarse_down = jnp.sum(
+        shares_out.reshape(ranks, -1, D_C).astype(jnp.float32), axis=0
+    )
     dx_coarse_tok = norm_backward(coarse_tokens, coarse_inverse, coarse_factor, coarse_down)
-    fine_qkv_sum, fine_out_sum = lax.psum((grad_qkv_local, grad_out_local), ("batch", "gy", "gx"))
-    coarse_qkv_sum, coarse_out_sum = lax.psum((coarse_qkv_local, coarse_out_local), "batch")
+    fine_local = jnp.concatenate([grad_qkv_local, grad_out_local], axis=1).astype(jnp.bfloat16)
+    everywhere = ("batch", "gy", "gx")
+    if D_F % lax.axis_size(everywhere) == 0:
+        fine_part = lax.psum_scatter(fine_local, everywhere, scatter_dimension=0, tiled=True)
+        fine_all = lax.all_gather(fine_part, everywhere, axis=0, tiled=True)
+    else:
+        fine_all = lax.psum(fine_local, everywhere)
+    fine_qkv_sum, fine_out_sum = fine_all[:, : 3 * D_F], fine_all[:, 3 * D_F :]
+    coarse_local = jnp.concatenate([coarse_qkv_local, coarse_out_local[None]], axis=0)
+    coarse_sum = batch_sum(coarse_local.astype(jnp.bfloat16))
+    coarse_qkv_sum, coarse_out_sum = coarse_sum[:3], coarse_sum[3]
     return (
         dx_picture[None],
         dx_coarse_tok.reshape(x_coarse.shape),

time: 206 us -> 262 us (1.27)
  waiting for transfers between devices: 10.3 us -> 136 us
  blocking collectives: 125 us -> 38 us
  starting transfers between devices: 18.6 us -> 26.5 us
  local copies, waits for them, and re-layouts: 16.3 us -> 21.2 us
  other arithmetic: 8.66 us -> 11.4 us
    reduce_scatter x1, waiting for transfers between devices: 0.01 us -> 121 us  [local(): lax.psum_scatter(fine_local, everywhere, scatter_dimension=0, tiled=True)]
    psum x2 -> x0, blocking collectives: 81.9 us -> none  [the longest x1 51.3 us: local(): lax.psum((grad_qkv_local, grad_out_local), ('batch', 'gy', 'gx'))]
    all_gather x2 -> x1, blocking collectives: 43.2 us -> 38 us  [local(): fine_all = lax.all_gather(fine_part, everywhere, axis=0, tiled=True)]
    all_to_all x0 -> x1, starting transfers between devices: none -> 4.18 us  [local(): lax.all_to_all(head_part.astype(jnp.bfloat16), ('gy', 'gx'), split_axis=0...]
    ppermute x2, waiting for transfers between devices: 2.78 us -> 6.77 us  [padded_2(): after = lax.ppermute(leading, axis, down)]
  transfers between devices with their start and end apart: 9 -> 12, of which waited for: 4 -> 6; matrix products, arithmetic and copies ran while one was open for 13% -> 15% of each run, Pallas kernels for 0% -> 0%
where the time goes in v1:
time: 262 us
  waiting for transfers between devices  136 us (52%)
  blocking collectives  38 us (15%)
  starting transfers between devices  26.5 us (10%)
  local copies, waits for them, and re-layouts  21.2 us (8%)
  between operations  16.9 us (6%)
  matrix products  11.9 us (5%)
  other arithmetic  11.4 us (4%)
    reduce_scatter x1, waiting for transfers between devices, local(): lax.psum_scatter(fine_local, everywhere, scatter_dimension=0, tiled=True)  121 us
    all_gather x1, blocking collectives, local(): fine_all = lax.all_gather(fine_part, everywhere, axis=0, tiled=True)  38 us
    ppermute x4, starting transfers between devices, shifted(): lax.ppermute(value, axis, [(source, source + steps) for source in range(l...  11.8 us
    dot_general x16, matrix products, contract(): jnp.einsum(pattern, first_op, second_op, preferred_element_type=jnp.float32)  8.8 us
    ppermute x4, waiting for transfers between devices, shifted(): lax.ppermute(value, axis, [(source, source + steps) for source in range(l...  7.59 us
    ppermute x2, waiting for transfers between devices, padded_2(): after = lax.ppermute(leading, axis, down)  6.77 us
    ppermute x2, starting transfers between devices, padded_2(): before = lax.ppermute(last, axis, up)  6.23 us
  transfers between devices with their start and end apart: 12, of which 6 were waited for; matrix products, arithmetic and copies ran while one was open for 15% of the time, Pallas kernels for 0%

profile of v1, /device:TPU:0, one launch (start us, length us, event | category | flops | bytes accessed | tf_op | source)
XLA Modules:
  0.0 261.7 jit_solution(9190628972273539497)
XLA Ops:
  8.1 0.8 reshape_squeeze.11
  8.9 0.8 reshape_squeeze.10
  9.7 0.6 pad_maximum_fusion.8
  11.1 1.0 fusion.34
  12.2 0.5 copy-done.12
  12.7 0.7 add_multiply_fusion.1
  13.4 1.0 fusion.26
  14.5 1.3 convolution_convert_fusion.1
  15.8 4.9 %collective-permute-start = (bf16[1,3,32,512]{3,2,1,0:T(8,128)(2,1)S(1)}, bf16[1,3,32,512]{3,2,1,0:T(8,128)(2,1)S(1)}, u32[]{:S(2)}, u32[]{:S(2)}) collective-permute-start(bf16[1,3,32,512]{3,2,1,0:T(8,128)(2,1)S(1)} %get-tuple-element.72), channel_id=1, source_target_pairs={{0,4},{4,8},{8,12},{1,5},{5,9},{9,13},{2,6},{6,10},{10,14},{3,7},{... | collective-permute-start | bytes 294920 | tf_op jit(solution)/shard_map/ppermute | solution.py:27
  20.7 1.3 collective-permute-start.1
  22.9 4.7 %collective-permute-done.1 = bf16[1,3,32,512]{3,2,1,0:T(8,128)(2,1)S(1)} collective-permute-done((bf16[1,3,32,512]{3,2,1,0:T(8,128)(2,1)S(1)}, bf16[1,3,32,512]{3,2,1,0:T(8,128)(2,1)S(1)}, u32[]{:S(2)}, u32[]{:S(2)}) %collective-permute-start.1) | collective-permute-done | bytes 98336 | tf_op jit(solution)/shard_map/ppermute | solution.py:28
  27.6 1.3 collective-permute-start.2
  28.9 1.3 collective-permute-start.3
  30.2 0.7 add_multiply_fusion
  31.7 2.1 collective-permute-done.3
  34.3 0.7 copy.40
  35.2 0.3 copy.41
  35.9 0.5 fusion.75
  36.3 0.4 exponential_reduce_fusion
  36.7 1.1 fusion.4
  37.9 0.6 multiply_reduce_fusion
  38.5 0.4 convolution_bitcast_fusion.1
  38.9 0.4 multiply_convert_fusion
  39.5 1.3 convolution_bitcast_fusion.2
  41.2 0.7 copy.56
  41.9 2.0 copy.51
  44.0 2.0 concatenate.68
  45.9 1.1 copy.53
  47.0 1.9 concatenate.69
  49.1 0.9 copy-done.2
  50.3 0.4 fusion.68
  50.7 0.4 add_bitcast_fusion
  51.2 1.0 copy.54
  52.2 0.7 fusion.69
  52.9 5.4 %collective-permute-start.4 = (f32[14,3,512]{2,1,0:T(4,128)}, f32[14,3,512]{2,1,0:T(4,128)}, u32[]{:S(2)}, u32[]{:S(2)}) collective-permute-start(f32[14,3,512]{2,1,0:T(4,128)} %get-tuple-element.61), channel_id=1, source_target_pairs={{0,1},{1,2},{2,3},{4,5},{5,6},{6,7},{8,9},{9,10},{10,11},{12,13},{... | collective-permute-start | bytes 258056 | tf_op jit(solution)/shard_map/ppermute | solution.py:36
  58.3 0.9 convolution_convert_fusion.4
  59.7 1.3 collective-permute-start.5
  61.1 0.9 slice_add_fusion.3
  62.0 0.4 scatter-add.14
  62.4 0.6 collective-permute-done.5
  63.0 0.3 scatter-add.15
  63.4 3.9 %collective-permute-start.6 = (f32[3,32,512]{2,1,0:T(8,128)S(1)}, f32[3,32,512]{2,1,0:T(8,128)S(1)}, u32[]{:S(2)}, u32[]{:S(2)}) collective-permute-start(f32[3,32,512]{2,1,0:T(8,128)S(1)} %get-tuple-element.63), channel_id=1, source_target_pairs={{0,4},{4,8},{8,12},{1,5},{5,9},{9,13},{2,6},{6,10},{10,14},{3,7},{... | collective-permute-start | bytes 589832 | tf_op jit(solution)/shard_map/ppermute | solution.py:36
  67.3 1.3 collective-permute-start.7
  68.6 2.5 collective-permute-done.6
  71.2 4.5 %collective-permute-done.7 = f32[3,32,512]{2,1,0:T(8,128)S(1)} collective-permute-done((f32[3,32,512]{2,1,0:T(8,128)S(1)}, f32[3,32,512]{2,1,0:T(8,128)S(1)}, u32[]{:S(2)}, u32[]{:S(2)}) %collective-permute-start.7) | collective-permute-done | bytes 196640 | tf_op jit(solution)/shard_map/ppermute | solution.py:36
  75.9 0.4 fusion.2
  76.3 0.4 copy-done.8
  76.7 0.9 pad_maximum_fusion.2
  77.6 0.4 fusion.35
  78.0 1.3 fusion.13
  79.4 1.4 fusion.7
  82.3 1.1 fusion.1
  83.5 4.2 %all-to-all-start = ((bf16[16,16,1024]{2,1,0:T(8,128)(2,1)}), bf16[16,16,1024]{2,1,0:T(8,128)(2,1)S(1)}, u32[]{:S(2)}, u32[]{:S(2)}) async-start(bf16[16,16,1024]{2,1,0:T(8,128)(2,1)} %bitcast.36), calls=%async_computation | async-start | bytes 1048576 | tf_op jit(solution)/shard_map/all_to_all | solution.py:303
  87.7 0.4 fusion.6
  88.0 0.4 convolution_convert_fusion
  88.5 1.6 collective-permute-start.8
  90.1 0.8 fusion.40
  90.9 121.3 %reduce-scatter.2.cloned.1.call-done = bf16[8,1024]{1,0:T(8,128)(2,1)} async-done(((bf16[256,1024]{1,0:T(8,128)(2,1)}), bf16[8,1024]{1,0:T(8,128)(2,1)}) %reduce-scatter.2.cloned.1.call-update) | async-done | bytes 16400 | tf_op jit(solution)/shard_map/reduce_scatter | solution.py:314
  212.1 38.0 %all_gather.7 = bf16[256,1024]{1,0:T(8,128)(2,1)S(1)} all-gather(bf16[8,1024]{1,0:T(8,128)(2,1)} %reduce-scatter.2.cloned.1.call-done), channel_id=1, replica_groups=mesh['batch'=2,'gy'=4,'gx'=4] {'batch','gy','gx'}, dimensions={0}, use_global_device_ids=true | all-gather | bytes 540672 | tf_op jit(solution)/shard_map/all_gather | solution.py:315
  250.1 0.7 slice.299
  250.8 0.8 slice.298
  251.8 0.8 slice.300
  252.6 0.7 slice_bitcast_fusion.1
  253.5 0.7 fusion.48
  (111 shorter events, 6.8 us)
Async XLA Ops:
  8.0 71.4 %copy-start = (bf16[3,64,1024]{2,1,0:T(8,128)(2,1)S(1)}, bf16[3,64,1024]{2,1,0:T(8,128)(2,1)}, u32[]{:S(2)}) copy-start(bf16[3,64,1024]{2,1,0:T(8,128)(2,1)} %param.28) | copy-start | bytes 1179652
  8.0 14.5 %copy-start.11 = (bf16[256,256]{1,0:T(8,128)(2,1)S(1)}, bf16[256,256]{1,0:T(8,128)(2,1)}, u32[]{:S(2)}) copy-start(bf16[256,256]{1,0:T(8,128)(2,1)} %param.27) | copy-start | bytes 393220
  8.0 14.5 %copy-start.6 = (bf16[1,8,32,256]{3,2,1,0:T(8,128)(2,1)S(1)}, bf16[1,8,32,256]{3,2,1,0:T(8,128)(2,1)}, u32[]{:S(2)}) copy-start(bf16[1,8,32,256]{3,2,1,0:T(8,128)(2,1)} %param.20) | copy-start | bytes 393220
  8.0 70.0 %all-gather.2.cloned.1.call-start = ((), (), s32[]{:S(2)}) async-start(), calls=%async_computation.2 | async-start | bytes 1114112 | tf_op jit(solution)/shard_map/all_gather | solution.py:274
  10.4 201.8 %reduce-scatter.2.cloned.1.call-start = ((), (), s32[]{:S(2)}) async-start(), calls=%async_computation.3 | async-start | bytes 540672 | tf_op jit(solution)/shard_map/reduce_scatter | solution.py:314
  12.1 0.6 copy-start.12
  13.4 2.3 copy-start.15
  14.4 15.8 %copy-start.17 = (f32[1024]{0:T(1024)S(1)}, f32[1024]{0:T(1024)}, u32[]{:S(2)}) copy-start(f32[1024]{0:T(1024)} %param.25) | copy-start | bytes 12292
  15.8 7.1 %collective-permute-start = (bf16[1,3,32,512]{3,2,1,0:T(8,128)(2,1)S(1)}, bf16[1,3,32,512]{3,2,1,0:T(8,128)(2,1)S(1)}, u32[]{:S(2)}, u32[]{:S(2)}) collective-permute-start(bf16[1,3,32,512]{3,2,1,0:T(8,128)(2,1)S(1)} %get-tuple-element.72), channel_id=1, source_target_pairs={{0,4},{4,8},{8,12},{1,5},{5,9},{9,13},{2,6},{6,10},{10,14},{3,7},{... | collective-permute-start | bytes 294920 | tf_op jit(solution)/shard_map/ppermute | solution.py:27
  20.7 6.9 %collective-permute-start.1 = (bf16[1,3,32,512]{3,2,1,0:T(8,128)(2,1)S(1)}, bf16[1,3,32,512]{3,2,1,0:T(8,128)(2,1)S(1)}, u32[]{:S(2)}, u32[]{:S(2)}) collective-permute-start(bf16[1,3,32,512]{3,2,1,0:T(8,128)(2,1)S(1)} %get-tuple-element.73), channel_id=1, source_target_pairs={{4,0},{8,4},{12,8},{5,1},{9,5},{13,9},{6,2},{10,6},{14,10},{7,3},{... | collective-permute-start | bytes 294920 | tf_op jit(solution)/shard_map/ppermute | solution.py:28
  27.6 4.0 %collective-permute-start.2 = (bf16[1,14,3,512]{3,2,1,0:T(4,128)(2,1)S(1)}, bf16[1,14,3,512]{3,2,1,0:T(4,128)(2,1)S(1)}, u32[]{:S(2)}, u32[]{:S(2)}) collective-permute-start(bf16[1,14,3,512]{3,2,1,0:T(4,128)(2,1)S(1)} %get-tuple-element.70), channel_id=1, source_target_pairs={{0,1},{1,2},{2,3},{4,5},{5,6},{6,7},{8,9},{9,10},{10,11},{12,13},{... | collective-permute-start | bytes 129032 | tf_op jit(solution)/shard_map/ppermute | solution.py:27
  28.9 4.9 %collective-permute-start.3 = (bf16[1,14,3,512]{3,2,1,0:T(4,128)(2,1)S(1)}, bf16[1,14,3,512]{3,2,1,0:T(4,128)(2,1)S(1)}, u32[]{:S(2)}, u32[]{:S(2)}) collective-permute-start(bf16[1,14,3,512]{3,2,1,0:T(4,128)(2,1)S(1)} %get-tuple-element.71), channel_id=1, source_target_pairs={{1,0},{2,1},{3,2},{5,4},{6,5},{7,6},{9,8},{10,9},{11,10},{13,12},{... | collective-permute-start | bytes 129032 | tf_op jit(solution)/shard_map/ppermute | solution.py:28
  39.2 1.6 copy-start.5
  47.0 2.0 copy-start.1
  48.9 1.1 copy-start.2
  51.2 7.1 %copy-start.7 = (bf16[1,8,4,8,256]{4,3,2,1,0:T(8,128)(2,1)S(1)}, bf16[1,8,4,8,256]{4,3,2,1,0:T(8,128)(2,1)}, u32[]{:S(2)}) copy-start(bf16[1,8,4,8,256]{4,3,2,1,0:T(8,128)(2,1)} %copy.56) | copy-start | bytes 393220
  52.9 8.1 %collective-permute-start.4 = (f32[14,3,512]{2,1,0:T(4,128)}, f32[14,3,512]{2,1,0:T(4,128)}, u32[]{:S(2)}, u32[]{:S(2)}) collective-permute-start(f32[14,3,512]{2,1,0:T(4,128)} %get-tuple-element.61), channel_id=1, source_target_pairs={{0,1},{1,2},{2,3},{4,5},{5,6},{6,7},{8,9},{9,10},{10,11},{12,13},{... | collective-permute-start | bytes 258056 | tf_op jit(solution)/shard_map/ppermute | solution.py:36
  59.7 3.2 %collective-permute-start.5 = (f32[14,3,512]{2,1,0:T(4,128)S(1)}, f32[14,3,512]{2,1,0:T(4,128)S(1)}, u32[]{:S(2)}, u32[]{:S(2)}) collective-permute-start(f32[14,3,512]{2,1,0:T(4,128)S(1)} %get-tuple-element.60), channel_id=1, source_target_pairs={{1,0},{2,1},{3,2},{5,4},{6,5},{7,6},{9,8},{10,9},{11,10},{13,12},{... | collective-permute-start | bytes 258056 | tf_op jit(solution)/shard_map/ppermute | solution.py:36
  63.4 12.4 %copy-start.3 = (bf16[1,8,32,256]{3,2,1,0:T(8,128)(2,1)S(1)}, bf16[1,8,32,256]{3,2,1,0:T(8,128)(2,1)}, u32[]{:S(2)}) copy-start(bf16[1,8,32,256]{3,2,1,0:T(8,128)(2,1)} %param.19) | copy-start | bytes 393220
  63.4 12.4 %copy-start.13 = (f32[8,32]{1,0:T(8,128)S(1)}, f32[8,32]{1,0:T(8,128)}, u32[]{:S(2)}) copy-start(f32[8,32]{1,0:T(8,128)} %copy-done.12) | copy-start | bytes 3076
  63.4 12.4 %copy-start.16 = (f32[256]{0:T(256)S(1)}, f32[256]{0:T(256)}, u32[]{:S(2)}) copy-start(f32[256]{0:T(256)} %copy-done.15) | copy-start | bytes 3076
  63.4 7.8 %collective-permute-start.6 = (f32[3,32,512]{2,1,0:T(8,128)S(1)}, f32[3,32,512]{2,1,0:T(8,128)S(1)}, u32[]{:S(2)}, u32[]{:S(2)}) collective-permute-start(f32[3,32,512]{2,1,0:T(8,128)S(1)} %get-tuple-element.63), channel_id=1, source_target_pairs={{0,4},{4,8},{8,12},{1,5},{5,9},{9,13},{2,6},{6,10},{10,14},{3,7},{... | collective-permute-start | bytes 589832 | tf_op jit(solution)/shard_map/ppermute | solution.py:36
  67.3 8.4 %collective-permute-start.7 = (f32[3,32,512]{2,1,0:T(8,128)S(1)}, f32[3,32,512]{2,1,0:T(8,128)S(1)}, u32[]{:S(2)}, u32[]{:S(2)}) collective-permute-start(f32[3,32,512]{2,1,0:T(8,128)S(1)} %get-tuple-element.62), channel_id=1, source_target_pairs={{4,0},{8,4},{12,8},{5,1},{9,5},{13,9},{6,2},{10,6},{14,10},{7,3},{... | collective-permute-start | bytes 589832 | tf_op jit(solution)/shard_map/ppermute | solution.py:36
  75.8 0.9 copy-start.8
  75.9 1.7 copy-start.9
  77.6 1.8 copy-start.14
  78.0 3.2 %copy-start.18 = (bf16[64,1024]{1,0:T(8,128)(2,1)S(1)}, bf16[64,1024]{1,0:T(8,128)(2,1)}, u32[]{:S(2)}) copy-start(bf16[64,1024]{1,0:T(8,128)(2,1)} %param.29) | copy-start | bytes 393220
  78.0 3.2 %copy-start.4 = (bf16[256,2048]{1,0:T(8,128)(2,1)S(1)}, bf16[256,2048]{1,0:T(8,128)(2,1)}, u32[]{:S(2)}) copy-start(bf16[256,2048]{1,0:T(8,128)(2,1)} %all-gather.2.cloned.1.call-done) | copy-start | bytes 3145732
  83.5 169.8 %all-to-all-start = ((bf16[16,16,1024]{2,1,0:T(8,128)(2,1)}), bf16[16,16,1024]{2,1,0:T(8,128)(2,1)S(1)}, u32[]{:S(2)}, u32[]{:S(2)}) async-start(bf16[16,16,1024]{2,1,0:T(8,128)(2,1)} %bitcast.36), calls=%async_computation | async-start | bytes 1048576 | tf_op jit(solution)/shard_map/all_to_all | solution.py:303
  88.5 163.1 %collective-permute-start.8 = (bf16[4,64,1024]{2,1,0:T(8,128)(2,1)S(1)}, bf16[4,64,1024]{2,1,0:T(8,128)(2,1)S(1)}, u32[]{:S(2)}, u32[]{:S(2)}) collective-permute-start(bf16[4,64,1024]{2,1,0:T(8,128)(2,1)S(1)} %pad_maximum_fusion.3), channel_id=1, source_target_pairs={{0,16},{16,0},{1,17},{17,1},{2,18},{18,2},{3,19},{19,3},{4,20},{20... | collective-permute-start | bytes 1572872 | tf_op jit(solution)/shard_map/ppermute | solution.py:186
  251.6 1.8 copy-start.10
Sparse Core Ops, SparseCore 0:
  11.6 40.7 all-gather.1
Sparse Core Ops, SparseCore 1:
  78.1 134.0 reduce-scatter.1
